TPU v7x, 512 devices: a whole 4x8x8 slice. The times are simulated.
512 devices in a mesh: stratum: 16 (over y, z_hi), user: 32 (over x, z_lo, core).
Axes of the slice: x: 4, y: 8, z: 8 (z_hi: 2, z_lo: 4; z = z_hi * 4 + z_lo), core: 2. Of those that a mesh axis runs over, the one named last changes fastest.
Arguments:
- users: bfloat16 [524288, 512], P(('stratum', 'user')), may hold values from -6 to 6
- items: float32 [4096, 512], P(('stratum', 'user')), may hold values from -6 to 6
- momentum: float32 [4096, 512], P(('stratum', 'user')), may hold values from -30 to 30
- ratings: bfloat16 [524288, 4, 256], P(('stratum', 'user')), may hold values from -6.25 to 6.25, as said below
Outputs:
- new_users: bfloat16 [524288, 512], P(('stratum', 'user'))
- new_items: float32 [4096, 512], P(('stratum', 'user'))
- new_momentum: float32 [4096, 512], P(('stratum', 'user'))
Inputs may be any that keep to these rules, and one draw needn't show every extreme that they name: `ratings`: an entry equal to zero marks an unobserved rating; every observed rating has magnitude 0.25 or more.
All inputs are finite; a program needn't handle non-finite values.
Results may differ from a plain program's by a relative error of at most 0.013.
The roundings to bfloat16 on the way count: a program that leaves them out, or rounds other values in their place, can miss the bound.
Values may be sent and summed in bfloat16 or wider, within the bound.
A program may use at most 64 MiB of HBM per device.

v0:
```python
import jax
import jax.numpy as jnp
from jax import lax
from jax.sharding import PartitionSpec as P

R = 512
STEPS = 4


user_rate = 1.0
item_rate = 0.04
inertia = 0.6


def in_order(tiles, dim):
    dims = list(tiles.shape[1:])
    dims[dim] *= tiles.shape[0]
    return jnp.moveaxis(tiles, 0, dim).reshape(dims)


def copy_for_each(x, axis):
    size = lax.axis_size(axis)
    return lax.all_to_all(jnp.broadcast_to(x[None], (size, *x.shape)), axis, 0, 0, tiled=True)


def collect(x, axis, dim):
    return in_order(copy_for_each(x, axis), dim)


def cut_along(x, dim, size):
    before, after = (x.shape[:dim], x.shape[dim + 1 :])
    return jnp.moveaxis(x.reshape(*before, size, -1, *after), dim, 0)


def summed_on_arrival(x, axis, dim):
    size = lax.axis_size(axis)
    tiles = lax.all_to_all(cut_along(x, dim, size), axis, 0, 0, tiled=True)
    return jnp.sum(tiles, axis=0)


def shifted(block, axis, distance):
    devices = range(lax.axis_size(axis))
    route = [((i - distance) % len(devices), i) for i in devices]
    return lax.ppermute(block, axis, route)


def local(users, items, momentum, ratings):
    factor = R ** (-0.5)
    own_rows = items.shape[0]
    for step in range(STEPS):
        whole = collect(items.astype(jnp.bfloat16), "user", 0)
        tile = ratings[:, step, :]
        score = lax.dot_general(
            users, whole, (((1,), (1,)), ((), ())), preferred_element_type=jnp.float32
        )
        resid = jnp.where(tile != 0, score * factor - tile.astype(jnp.float32), 0.0).astype(
            jnp.bfloat16
        )
        previous = users

        def item_terms(start, count, resid=resid, previous=previous):
            return lax.dot_general(
                resid, previous, (((0,), (0,)), ((), ())), preferred_element_type=jnp.float32
            )

        grads = summed_on_arrival(
            item_terms(jnp.int32(0), own_rows * lax.axis_size("user")), "user", 0
        )
        change = jnp.dot(resid, whole, preferred_element_type=jnp.float32)
        users = (users.astype(jnp.float32) - user_rate * factor * change).astype(jnp.bfloat16)
        momentum = inertia * momentum + factor * grads
        items = items - item_rate * momentum
        items, momentum = shifted((items, momentum), "stratum", -1)
    return (users, items, momentum)


def solution(mesh):
    in_specs = (
        P(("stratum", "user"), None),
        P(("stratum", "user"), None),
        P(("stratum", "user"), None),
        P(("stratum", "user"), None, None),
    )
    out_specs = (
        P(("stratum", "user"), None),
        P(("stratum", "user"), None),
        P(("stratum", "user"), None),
    )
    return jax.shard_map(local, mesh=mesh, in_specs=in_specs, out_specs=out_specs, check_vma=False)
```

profile of v0, /device:TPU:1, one launch (start us, length us, event | category | flops | bytes accessed | tf_op | source)
XLA Modules:
  0.0 223.4 jit_solution(17617571519090849853)
XLA Ops:
  2.1 11.4 %all-to-all-start = ((bf16[32,8,512]{2,1,0:T(8,128)(2,1)}), bf16[32,8,512]{2,1,0:T(8,128)(2,1)S(1)}, u32[]{:S(2)}, u32[]{:S(2)}) async-start(bf16[32,8,512]{2,1,0:T(8,128)(2,1)} %broadcast_in_dim.15), calls=%async_computation | async-start | bytes 524288 | tf_op jit(solution)/shard_map/all_to_all | solution.py:23
  13.5 8.9 %fusion.20 = (bf16[1024,1,256]{2,1,0:T(2,128)(2,1)}, bf16[1024,1,256]{2,1,0:T(2,128)(2,1)}, bf16[1024,1,256]{2,1,0:T(2,128)(2,1)}, bf16[1024,1,256]{2,1,0:T(2,128)(2,1)S(1)}) fusion(bf16[1024,4,256]{2,1,0:T(4,128)(2,1)} %param.7), kind=kLoop, calls=%fused_computation.40 | loop fusion | bytes 4194304 | tf_op jit(solution)/shard_map/slice | solution.py:52
  22.4 2.4 %all-to-all-done = bf16[32,8,512]{2,1,0:T(8,128)(2,1)S(1)} async-done(((bf16[32,8,512]{2,1,0:T(8,128)(2,1)}), bf16[32,8,512]{2,1,0:T(8,128)(2,1)S(1)}, u32[]{:S(2)}, u32[]{:S(2)}) %all-to-all-start) | async-done | bytes 262176 | tf_op jit(solution)/shard_map/all_to_all | solution.py:23
  25.7 22.0 %all_to_all.40 = f32[32,8,512]{2,1,0:T(8,128)S(1)} all-to-all(f32[32,8,512]{2,1,0:T(8,128)S(1)} %convolution_bitcast_fusion.3), channel_id=1, replica_groups=mesh['stratum'=16,'user'=32] {'user'}, dimensions={0} | all-to-all | bytes 1048576 | tf_op jit(solution)/shard_map/all_to_all | solution.py:37
  47.8 10.8 %collective-permute-start = (f32[8,512]{1,0:T(8,128)S(1)}, f32[8,512]{1,0:T(8,128)S(1)}, u32[]{:S(2)}, u32[]{:S(2)}) collective-permute-start(f32[8,512]{1,0:T(8,128)S(1)} %get-tuple-element.9), channel_id=1, source_target_pairs={{32,0},{64,32},{96,64},{128,96},{160,128},{192,160},{224,192},{256... | collective-permute-start | bytes 49160 | tf_op jit(solution)/shard_map/ppermute | solution.py:44
  60.2 4.6 %all-to-all-start.2 = ((bf16[32,8,512]{2,1,0:T(8,128)(2,1)}), bf16[32,8,512]{2,1,0:T(8,128)(2,1)S(1)}, u32[]{:S(2)}, u32[]{:S(2)}) async-start(bf16[32,8,512]{2,1,0:T(8,128)(2,1)} %broadcast_in_dim.17), calls=%async_computation.2 | async-start | bytes 524288 | tf_op jit(solution)/shard_map/all_to_all | solution.py:23
  65.2 10.9 %all-to-all-done.2 = bf16[32,8,512]{2,1,0:T(8,128)(2,1)S(1)} async-done(((bf16[32,8,512]{2,1,0:T(8,128)(2,1)}), bf16[32,8,512]{2,1,0:T(8,128)(2,1)S(1)}, u32[]{:S(2)}, u32[]{:S(2)}) %all-to-all-start.2) | async-done | bytes 262176 | tf_op jit(solution)/shard_map/all_to_all | solution.py:23
  76.1 1.7 fusion.9
  77.8 1.3 convolution_bitcast_fusion.2
  79.1 3.7 %all-to-all-start.3 = ((f32[32,8,512]{2,1,0:T(8,128)}), f32[32,8,512]{2,1,0:T(8,128)S(1)}, u32[]{:S(2)}, u32[]{:S(2)}) async-start(f32[32,8,512]{2,1,0:T(8,128)} %convolution_bitcast_fusion.2), calls=%async_computation.3 | async-start | bytes 1048576 | tf_op jit(solution)/shard_map/all_to_all | solution.py:37
  82.8 9.9 %collective-permute-start.1 = (f32[8,512]{1,0:T(8,128)S(1)}, f32[8,512]{1,0:T(8,128)S(1)}, u32[]{:S(2)}, u32[]{:S(2)}) collective-permute-start(f32[8,512]{1,0:T(8,128)S(1)} %get-tuple-element.10), channel_id=1, source_target_pairs={{32,0},{64,32},{96,64},{128,96},{160,128},{192,160},{224,192},{256... | collective-permute-start | bytes 49160 | tf_op jit(solution)/shard_map/ppermute | solution.py:44
  92.7 7.6 %all-to-all-done.3 = f32[32,8,512]{2,1,0:T(8,128)S(1)} async-done(((f32[32,8,512]{2,1,0:T(8,128)}), f32[32,8,512]{2,1,0:T(8,128)S(1)}, u32[]{:S(2)}, u32[]{:S(2)}) %all-to-all-start.3) | async-done | bytes 524320 | tf_op jit(solution)/shard_map/all_to_all | solution.py:37
  100.4 10.0 %collective-permute-start.2 = (f32[8,512]{1,0:T(8,128)S(1)}, f32[8,512]{1,0:T(8,128)S(1)}, u32[]{:S(2)}, u32[]{:S(2)}) collective-permute-start(f32[8,512]{1,0:T(8,128)S(1)} %get-tuple-element.7), channel_id=1, source_target_pairs={{32,0},{64,32},{96,64},{128,96},{160,128},{192,160},{224,192},{256... | collective-permute-start | bytes 49160 | tf_op jit(solution)/shard_map/ppermute | solution.py:44
  111.9 4.5 %all-to-all-start.4 = ((bf16[32,8,512]{2,1,0:T(8,128)(2,1)}), bf16[32,8,512]{2,1,0:T(8,128)(2,1)S(1)}, u32[]{:S(2)}, u32[]{:S(2)}) async-start(bf16[32,8,512]{2,1,0:T(8,128)(2,1)} %broadcast_in_dim.34), calls=%async_computation.4 | async-start | bytes 524288 | tf_op jit(solution)/shard_map/all_to_all | solution.py:23
  116.9 11.0 %all-to-all-done.4 = bf16[32,8,512]{2,1,0:T(8,128)(2,1)S(1)} async-done(((bf16[32,8,512]{2,1,0:T(8,128)(2,1)}), bf16[32,8,512]{2,1,0:T(8,128)(2,1)S(1)}, u32[]{:S(2)}, u32[]{:S(2)}) %all-to-all-start.4) | async-done | bytes 262176 | tf_op jit(solution)/shard_map/all_to_all | solution.py:23
  127.9 1.7 fusion.10
  129.6 1.3 convolution_bitcast_fusion.1
  130.8 3.7 %all-to-all-start.5 = ((f32[32,8,512]{2,1,0:T(8,128)}), f32[32,8,512]{2,1,0:T(8,128)S(1)}, u32[]{:S(2)}, u32[]{:S(2)}) async-start(f32[32,8,512]{2,1,0:T(8,128)} %convolution_bitcast_fusion.1), calls=%async_computation.5 | async-start | bytes 1048576 | tf_op jit(solution)/shard_map/all_to_all | solution.py:37
  134.5 9.9 %collective-permute-start.3 = (f32[8,512]{1,0:T(8,128)S(1)}, f32[8,512]{1,0:T(8,128)S(1)}, u32[]{:S(2)}, u32[]{:S(2)}) collective-permute-start(f32[8,512]{1,0:T(8,128)S(1)} %get-tuple-element.8), channel_id=1, source_target_pairs={{32,0},{64,32},{96,64},{128,96},{160,128},{192,160},{224,192},{256... | collective-permute-start | bytes 49160 | tf_op jit(solution)/shard_map/ppermute | solution.py:44
  144.5 7.6 %all-to-all-done.5 = f32[32,8,512]{2,1,0:T(8,128)S(1)} async-done(((f32[32,8,512]{2,1,0:T(8,128)}), f32[32,8,512]{2,1,0:T(8,128)S(1)}, u32[]{:S(2)}, u32[]{:S(2)}) %all-to-all-start.5) | async-done | bytes 524320 | tf_op jit(solution)/shard_map/all_to_all | solution.py:37
  152.1 10.0 %collective-permute-start.4 = (f32[8,512]{1,0:T(8,128)S(1)}, f32[8,512]{1,0:T(8,128)S(1)}, u32[]{:S(2)}, u32[]{:S(2)}) collective-permute-start(f32[8,512]{1,0:T(8,128)S(1)} %get-tuple-element.5), channel_id=1, source_target_pairs={{32,0},{64,32},{96,64},{128,96},{160,128},{192,160},{224,192},{256... | collective-permute-start | bytes 49160 | tf_op jit(solution)/shard_map/ppermute | solution.py:44
  163.7 4.5 %all-to-all-start.6 = ((bf16[32,8,512]{2,1,0:T(8,128)(2,1)}), bf16[32,8,512]{2,1,0:T(8,128)(2,1)S(1)}, u32[]{:S(2)}, u32[]{:S(2)}) async-start(bf16[32,8,512]{2,1,0:T(8,128)(2,1)} %broadcast_in_dim.35), calls=%async_computation.6 | async-start | bytes 524288 | tf_op jit(solution)/shard_map/all_to_all | solution.py:23
  168.7 11.0 %all-to-all-done.6 = bf16[32,8,512]{2,1,0:T(8,128)(2,1)S(1)} async-done(((bf16[32,8,512]{2,1,0:T(8,128)(2,1)}), bf16[32,8,512]{2,1,0:T(8,128)(2,1)S(1)}, u32[]{:S(2)}, u32[]{:S(2)}) %all-to-all-start.6) | async-done | bytes 262176 | tf_op jit(solution)/shard_map/all_to_all | solution.py:23
  179.6 1.7 fusion.11
  181.3 1.3 convolution_bitcast_fusion
  182.6 3.7 %all-to-all-start.7 = ((f32[32,8,512]{2,1,0:T(8,128)}), f32[32,8,512]{2,1,0:T(8,128)S(1)}, u32[]{:S(2)}, u32[]{:S(2)}) async-start(f32[32,8,512]{2,1,0:T(8,128)} %convolution_bitcast_fusion), calls=%async_computation.7 | async-start | bytes 1048576 | tf_op jit(solution)/shard_map/all_to_all | solution.py:37
  186.2 9.9 %collective-permute-start.5 = (f32[8,512]{1,0:T(8,128)S(1)}, f32[8,512]{1,0:T(8,128)S(1)}, u32[]{:S(2)}, u32[]{:S(2)}) collective-permute-start(f32[8,512]{1,0:T(8,128)S(1)} %get-tuple-element.6), channel_id=1, source_target_pairs={{32,0},{64,32},{96,64},{128,96},{160,128},{192,160},{224,192},{256... | collective-permute-start | bytes 49160 | tf_op jit(solution)/shard_map/ppermute | solution.py:44
  196.2 7.6 %all-to-all-done.7 = f32[32,8,512]{2,1,0:T(8,128)S(1)} async-done(((f32[32,8,512]{2,1,0:T(8,128)}), f32[32,8,512]{2,1,0:T(8,128)S(1)}, u32[]{:S(2)}, u32[]{:S(2)}) %all-to-all-start.7) | async-done | bytes 524320 | tf_op jit(solution)/shard_map/all_to_all | solution.py:37
  203.9 10.0 %collective-permute-start.6 = (f32[8,512]{1,0:T(8,128)S(1)}, f32[8,512]{1,0:T(8,128)S(1)}, u32[]{:S(2)}, u32[]{:S(2)}) collective-permute-start(f32[8,512]{1,0:T(8,128)S(1)} %get-tuple-element.3), channel_id=1, source_target_pairs={{32,0},{64,32},{96,64},{128,96},{160,128},{192,160},{224,192},{256... | collective-permute-start | bytes 49160 | tf_op jit(solution)/shard_map/ppermute | solution.py:44
  213.8 2.0 collective-permute-start.7
  215.8 1.4 subtract_convert_fusion
  217.2 5.0 %collective-permute-done.7 = f32[8,512]{1,0:T(8,128)S(1)} collective-permute-done((f32[8,512]{1,0:T(8,128)S(1)}, f32[8,512]{1,0:T(8,128)S(1)}, u32[]{:S(2)}, u32[]{:S(2)}) %collective-permute-start.7) | collective-permute-done | bytes 16416 | tf_op jit(solution)/shard_map/ppermute | solution.py:44
  (36 shorter events, 9.9 us)
Async XLA Ops:
  2.1 22.7 %all-to-all-start = ((bf16[32,8,512]{2,1,0:T(8,128)(2,1)}), bf16[32,8,512]{2,1,0:T(8,128)(2,1)S(1)}, u32[]{:S(2)}, u32[]{:S(2)}) async-start(bf16[32,8,512]{2,1,0:T(8,128)(2,1)} %broadcast_in_dim.15), calls=%async_computation | async-start | bytes 524288 | tf_op jit(solution)/shard_map/all_to_all | solution.py:23
  13.5 11.3 %copy-start = (bf16[1024,512]{1,0:T(8,128)(2,1)S(1)}, bf16[1024,512]{1,0:T(8,128)(2,1)}, u32[]{:S(2)}) copy-start(bf16[1024,512]{1,0:T(8,128)(2,1)} %param.4) | copy-start | bytes 3145732
  25.2 22.5 %copy-start.1 = (f32[8,512]{1,0:T(8,128)S(1)}, f32[8,512]{1,0:T(8,128)}, u32[]{:S(2)}) copy-start(f32[8,512]{1,0:T(8,128)} %param.5) | copy-start | bytes 49156
  25.2 22.5 %copy-start.2 = (f32[8,512]{1,0:T(8,128)S(1)}, f32[8,512]{1,0:T(8,128)}, u32[]{:S(2)}) copy-start(f32[8,512]{1,0:T(8,128)} %param.6) | copy-start | bytes 49156
  47.8 11.7 %collective-permute-start = (f32[8,512]{1,0:T(8,128)S(1)}, f32[8,512]{1,0:T(8,128)S(1)}, u32[]{:S(2)}, u32[]{:S(2)}) collective-permute-start(f32[8,512]{1,0:T(8,128)S(1)} %get-tuple-element.9), channel_id=1, source_target_pairs={{32,0},{64,32},{96,64},{128,96},{160,128},{192,160},{224,192},{256... | collective-permute-start | bytes 49160 | tf_op jit(solution)/shard_map/ppermute | solution.py:44
  60.2 15.9 %all-to-all-start.2 = ((bf16[32,8,512]{2,1,0:T(8,128)(2,1)}), bf16[32,8,512]{2,1,0:T(8,128)(2,1)S(1)}, u32[]{:S(2)}, u32[]{:S(2)}) async-start(bf16[32,8,512]{2,1,0:T(8,128)(2,1)} %broadcast_in_dim.17), calls=%async_computation.2 | async-start | bytes 524288 | tf_op jit(solution)/shard_map/all_to_all | solution.py:23
  79.1 21.2 %all-to-all-start.3 = ((f32[32,8,512]{2,1,0:T(8,128)}), f32[32,8,512]{2,1,0:T(8,128)S(1)}, u32[]{:S(2)}, u32[]{:S(2)}) async-start(f32[32,8,512]{2,1,0:T(8,128)} %convolution_bitcast_fusion.2), calls=%async_computation.3 | async-start | bytes 1048576 | tf_op jit(solution)/shard_map/all_to_all | solution.py:37
  82.8 17.6 %collective-permute-start.1 = (f32[8,512]{1,0:T(8,128)S(1)}, f32[8,512]{1,0:T(8,128)S(1)}, u32[]{:S(2)}, u32[]{:S(2)}) collective-permute-start(f32[8,512]{1,0:T(8,128)S(1)} %get-tuple-element.10), channel_id=1, source_target_pairs={{32,0},{64,32},{96,64},{128,96},{160,128},{192,160},{224,192},{256... | collective-permute-start | bytes 49160 | tf_op jit(solution)/shard_map/ppermute | solution.py:44
  100.4 10.8 %collective-permute-start.2 = (f32[8,512]{1,0:T(8,128)S(1)}, f32[8,512]{1,0:T(8,128)S(1)}, u32[]{:S(2)}, u32[]{:S(2)}) collective-permute-start(f32[8,512]{1,0:T(8,128)S(1)} %get-tuple-element.7), channel_id=1, source_target_pairs={{32,0},{64,32},{96,64},{128,96},{160,128},{192,160},{224,192},{256... | collective-permute-start | bytes 49160 | tf_op jit(solution)/shard_map/ppermute | solution.py:44
  111.9 15.9 %all-to-all-start.4 = ((bf16[32,8,512]{2,1,0:T(8,128)(2,1)}), bf16[32,8,512]{2,1,0:T(8,128)(2,1)S(1)}, u32[]{:S(2)}, u32[]{:S(2)}) async-start(bf16[32,8,512]{2,1,0:T(8,128)(2,1)} %broadcast_in_dim.34), calls=%async_computation.4 | async-start | bytes 524288 | tf_op jit(solution)/shard_map/all_to_all | solution.py:23
  130.8 21.2 %all-to-all-start.5 = ((f32[32,8,512]{2,1,0:T(8,128)}), f32[32,8,512]{2,1,0:T(8,128)S(1)}, u32[]{:S(2)}, u32[]{:S(2)}) async-start(f32[32,8,512]{2,1,0:T(8,128)} %convolution_bitcast_fusion.1), calls=%async_computation.5 | async-start | bytes 1048576 | tf_op jit(solution)/shard_map/all_to_all | solution.py:37
  134.5 17.6 %collective-permute-start.3 = (f32[8,512]{1,0:T(8,128)S(1)}, f32[8,512]{1,0:T(8,128)S(1)}, u32[]{:S(2)}, u32[]{:S(2)}) collective-permute-start(f32[8,512]{1,0:T(8,128)S(1)} %get-tuple-element.8), channel_id=1, source_target_pairs={{32,0},{64,32},{96,64},{128,96},{160,128},{192,160},{224,192},{256... | collective-permute-start | bytes 49160 | tf_op jit(solution)/shard_map/ppermute | solution.py:44
  152.1 10.8 %collective-permute-start.4 = (f32[8,512]{1,0:T(8,128)S(1)}, f32[8,512]{1,0:T(8,128)S(1)}, u32[]{:S(2)}, u32[]{:S(2)}) collective-permute-start(f32[8,512]{1,0:T(8,128)S(1)} %get-tuple-element.5), channel_id=1, source_target_pairs={{32,0},{64,32},{96,64},{128,96},{160,128},{192,160},{224,192},{256... | collective-permute-start | bytes 49160 | tf_op jit(solution)/shard_map/ppermute | solution.py:44
  163.7 15.9 %all-to-all-start.6 = ((bf16[32,8,512]{2,1,0:T(8,128)(2,1)}), bf16[32,8,512]{2,1,0:T(8,128)(2,1)S(1)}, u32[]{:S(2)}, u32[]{:S(2)}) async-start(bf16[32,8,512]{2,1,0:T(8,128)(2,1)} %broadcast_in_dim.35), calls=%async_computation.6 | async-start | bytes 524288 | tf_op jit(solution)/shard_map/all_to_all | solution.py:23
  182.6 21.2 %all-to-all-start.7 = ((f32[32,8,512]{2,1,0:T(8,128)}), f32[32,8,512]{2,1,0:T(8,128)S(1)}, u32[]{:S(2)}, u32[]{:S(2)}) async-start(f32[32,8,512]{2,1,0:T(8,128)} %convolution_bitcast_fusion), calls=%async_computation.7 | async-start | bytes 1048576 | tf_op jit(solution)/shard_map/all_to_all | solution.py:37
  186.2 17.6 %collective-permute-start.5 = (f32[8,512]{1,0:T(8,128)S(1)}, f32[8,512]{1,0:T(8,128)S(1)}, u32[]{:S(2)}, u32[]{:S(2)}) collective-permute-start(f32[8,512]{1,0:T(8,128)S(1)} %get-tuple-element.6), channel_id=1, source_target_pairs={{32,0},{64,32},{96,64},{128,96},{160,128},{192,160},{224,192},{256... | collective-permute-start | bytes 49160 | tf_op jit(solution)/shard_map/ppermute | solution.py:44
  203.9 13.4 %collective-permute-start.6 = (f32[8,512]{1,0:T(8,128)S(1)}, f32[8,512]{1,0:T(8,128)S(1)}, u32[]{:S(2)}, u32[]{:S(2)}) collective-permute-start(f32[8,512]{1,0:T(8,128)S(1)} %get-tuple-element.3), channel_id=1, source_target_pairs={{32,0},{64,32},{96,64},{128,96},{160,128},{192,160},{224,192},{256... | collective-permute-start | bytes 49160 | tf_op jit(solution)/shard_map/ppermute | solution.py:44
  213.8 8.4 %collective-permute-start.7 = (f32[8,512]{1,0:T(8,128)S(1)}, f32[8,512]{1,0:T(8,128)S(1)}, u32[]{:S(2)}, u32[]{:S(2)}) collective-permute-start(f32[8,512]{1,0:T(8,128)S(1)} %get-tuple-element.4), channel_id=1, source_target_pairs={{32,0},{64,32},{96,64},{128,96},{160,128},{192,160},{224,192},{256... | collective-permute-start | bytes 49160 | tf_op jit(solution)/shard_map/ppermute | solution.py:44
where the time goes:
time: 225 us; the launch traced here: 223 us
  starting transfers between devices  109 us (48%)
  waiting for transfers between devices  65.5 us (29%)
  blocking collectives  22 us (10%)
  local copies, waits for them, and re-layouts  13.1 us (6%)
  matrix products  12.5 us (6%)
    ppermute x8, starting transfers between devices, shifted(): return lax.ppermute(block, axis, route)  72.5 us
    all_to_all x4, waiting for transfers between devices, copy_for_each(): lax.all_to_all(jnp.broadcast_to(x[None], (size, *x.shape)), axis, 0, 0, t...  35.2 us
    all_to_all x4, starting transfers between devices, copy_for_each(): lax.all_to_all(jnp.broadcast_to(x[None], (size, *x.shape)), axis, 0, 0, t...  25 us
    all_to_all x3, waiting for transfers between devices, summed_on_arrival(): tiles = lax.all_to_all(cut_along(x, dim, size), axis, 0, 0, tiled=True)  22.8 us
    all_to_all x1, blocking collectives, summed_on_arrival(): tiles = lax.all_to_all(cut_along(x, dim, size), axis, 0, 0, tiled=True)  22 us
    all_to_all x3, starting transfers between devices, summed_on_arrival(): tiles = lax.all_to_all(cut_along(x, dim, size), axis, 0, 0, tiled=True)  11 us
    slice x1, local copies, waits for them, and re-layouts, local(): tile = ratings[:, step, :]  8.92 us
    ppermute x8, waiting for transfers between devices, shifted(): return lax.ppermute(block, axis, route)  7.54 us
  transfers between devices with their start and end apart: 15, of which 11 were waited for; matrix products, arithmetic and copies ran while one was open for 5% of the time, Pallas kernels for 0%

commit v1 on v0

v1 whole, which is shorter than its diff:
```python
import functools

import jax
import jax.numpy as jnp
from jax import lax
from jax.experimental import pallas as pl
from jax.experimental.pallas import tpu as pltpu
from jax.sharding import PartitionSpec as P

R = 512
HALF = 256
STEPS = 4
USERS = 1024
BLOCK = 256
X = 4
Z = 4
CHIPS = 16
ROWS = 16
STRATA = 16
FACTOR = R**-0.5
user_rate = 1.0
item_rate = 0.04
inertia = 0.6

MESH = pl.DeviceIdType.MESH
NT = (((1,), (1,)), ((), ()))
NN = (((1,), (0,)), ((), ()))
TILE = 256


def dot(a, b, dims):
    return lax.dot_general(a, b, dims, preferred_element_type=jnp.float32)


def kernel(
    users_in,
    items_in,
    momentum_in,
    ratings_in,
    users_out,
    items_out,
    momentum_out,
    u,
    raw,
    x,
    wide0,
    wide1,
    own,
    first,
    w,
    score,
    e,
    et,
    g,
    give,
    take,
    part,
    parts,
    state,
    fresh,
    load_sem,
    ag_send,
    ag_recv,
    fw_send,
    fw_recv,
    sib_send,
    sib_recv,
    rs_send,
    rs_recv,
    st_send,
    st_recv,
):
    s = lax.axis_index("stratum")
    me = lax.axis_index("user")
    core = me % 2
    chip = me // 2
    mx, mz = chip // Z, chip % Z
    prev = (s + STRATA - 1) % STRATA
    nxt = (s + 1) % STRATA
    other = 1 - core

    def chip_at(dx, dz):
        return ((mx + dx) % X) * Z + (mz + dz) % Z

    def dev(k, c):
        return k * 2 + c

    loads = [
        pltpu.make_async_copy(items_in, own.at[0], load_sem.at[0]),
        pltpu.make_async_copy(momentum_in, own.at[1], load_sem.at[1]),
        pltpu.make_async_copy(ratings_in, raw, load_sem.at[2]),
        pltpu.make_async_copy(users_in.at[:, pl.ds(0, HALF)], u.at[0], load_sem.at[3]),
        pltpu.make_async_copy(users_in.at[:, pl.ds(HALF, HALF)], u.at[1], load_sem.at[4]),
    ]
    for copy in loads:
        copy.start()

    far = [(dx, dz) for dx in (2, 1, 3, 0) for dz in (2, 1, 3, 0)]
    barrier = pltpu.get_barrier_semaphore()

    def hello(stratum, user):
        pl.semaphore_signal(barrier, inc=1, device_id=(stratum, user), device_id_type=MESH)

    for dx, dz in far:
        k = chip_at(dx, dz)
        hello(prev, dev(k, core))
        hello(nxt, dev(k, core))
        if (dx, dz) != (0, 0):
            hello(s, dev(k, core))
    hello(prev, dev(chip, other))
    hello(nxt, dev(chip, other))
    hello(s, dev(chip, other))
    loads[0].wait()
    loads[1].wait()
    first[core, chip] = jnp.concatenate([own[0, :, :HALF], own[0, :, HALF:]], axis=0).astype(
        jnp.bfloat16
    )
    pl.semaphore_wait(barrier, 3 * CHIPS + 2)

    def remote(src, dst, send, recv, stratum, user):
        return pltpu.make_async_remote_copy(
            src_ref=src,
            dst_ref=dst,
            send_sem=send,
            recv_sem=recv,
            device_id=(stratum, user),
            device_id_type=MESH,
        )

    def rows_of(k):
        return pl.ds(pl.multiple_of(k * ROWS, ROWS), ROWS)

    def spread(t, place):
        sends = []
        mine = place(core, chip)
        for dx, dz in far[:-1]:
            k = chip_at(dx, dz)
            sends.append(
                remote(mine, mine, ag_send.at[t, dx * Z + dz], ag_recv.at[t, chip], s, dev(k, core))
            )
            sends[-1].start()
        passed = []

        def pass_on(k, slot):
            piece = place(core, k)
            passed.append(
                remote(piece, piece, fw_send.at[t, slot], fw_recv.at[t, k], s, dev(chip, other))
            )
            passed[-1].start()

        pass_on(chip, 0)
        return sends, passed, pass_on

    def collect(t, place, pass_on):
        for slot, (dx, dz) in enumerate(far[:-1][::-1]):
            k = chip_at(dx, dz)
            piece = place(core, k)
            remote(piece, piece, ag_send.at[t, 0], ag_recv.at[t, k], s, me).wait_recv()
            pass_on(k, slot + 1)

    def collect_passed(t, place):
        for dx, dz in far[::-1]:
            k = chip_at(dx, dz)
            piece = place(other, k)
            remote(piece, piece, fw_send.at[t, 0], fw_recv.at[t, k], s, me).wait_recv()

    def finish(sends):
        for copy in sends:
            copy.wait_send()

    def place_first(c, k):
        return first.at[c, k]

    sends, passed, pass_on = spread(0, place_first)
    moves = []
    for c in range(2):
        moves.append(
            remote(
                own.at[:, :, pl.ds(c * HALF, HALF)],
                state.at[0, :, pl.ds(pl.multiple_of(core * 8, 8), 8), :],
                st_send.at[0, c],
                st_recv.at[0, core],
                prev,
                dev(chip, c),
            )
        )
        moves[-1].start()

    loads[2].wait()

    def split(i, _):
        r = pl.ds(pl.multiple_of(i * 128, 128), 128)
        for h, wide in enumerate((wide0, wide1)):
            lanes = slice(h * 128, h * 128 + 128)
            wide[...] = raw[r, :, lanes].astype(jnp.float32).reshape(128 * STEPS, 128)
        for t in range(STEPS):
            for h, wide in enumerate((wide0, wide1)):
                lanes = slice(h * 128, h * 128 + 128)
                x[t, r, lanes] = wide[pl.ds(t, 128, stride=STEPS), :].astype(jnp.bfloat16)
        return 0

    lax.fori_loop(0, USERS // 128, split, 0)
    loads[3].wait()
    loads[4].wait()

    collect(0, place_first, pass_on)
    collect_passed(0, place_first)
    finish(sends + passed)
    pieces = [first[c].astype(jnp.float32).reshape(CHIPS, 2, 8, HALF) for c in range(2)]
    for h in range(2):
        w[0, h] = (
            jnp.concatenate([pieces[0][:, h : h + 1], pieces[1][:, h : h + 1]], axis=1)
            .reshape(BLOCK, HALF)
            .astype(jnp.bfloat16)
        )

    store = []
    for t in range(STEPS):
        last = t == STEPS - 1

        def place(c, k, t=t):
            return w.at[t, c, rows_of(k), :]

        tiles = [pl.ds(i * TILE, TILE) for i in range(USERS // TILE)]
        if t == 0:
            for r in tiles:
                score[r, :] = dot(u[core, r, :], w[t, core], NT)
        else:
            for r in tiles:
                score[r, :] = dot(u[core, r, :], w[t, core], NT)
            collect_passed(t, place)
            finish(sends + passed)
        for r in tiles:
            total = score[r, :] + dot(u[other, r, :], w[t, other], NT)
            tile = x[t, r, :].astype(jnp.float32)
            resid = jnp.where(tile != 0, total * FACTOR - tile, 0.0).astype(jnp.bfloat16)
            e[r, :] = resid
            et[:, r] = resid.T
        if last:
            for h in range(2):
                g[h] = dot(et[...], u[h], NN).reshape(CHIPS, 2, 8, HALF)

            def piece_for(c):
                both = [g[h, :, pl.ds(c, 1)] for h in range(2)]
                return jnp.concatenate(both, axis=1).reshape(BLOCK, HALF)

            give[t] = piece_for(other).astype(jnp.bfloat16)
        else:
            give[t] = dot(et[...], u[other], NN).astype(jnp.bfloat16)
        swap = remote(
            give.at[t], take.at[t], sib_send.at[t], sib_recv.at[t], s, dev(chip, other)
        )
        swap.start()
        if not last:
            g[0] = dot(et[...], u[core], NN).reshape(CHIPS, 2, 8, HALF)
        for h in range(2):
            for r in tiles:
                change = dot(e[r, :], w[t, h], NN)
                u[h, r, :] = (
                    u[h, r, :].astype(jnp.float32) - user_rate * FACTOR * change
                ).astype(jnp.bfloat16)
        if last:
            for h in range(2):
                store.append(
                    pltpu.make_async_copy(
                        u.at[h], users_out.at[:, pl.ds(h * HALF, HALF)], load_sem.at[3 + h]
                    )
                )
                store[-1].start()
        swap.wait_recv()
        mine = piece_for(core) if last else g[0].reshape(BLOCK, HALF)
        part[t] = (mine + take[t].astype(jnp.float32)).astype(jnp.bfloat16)
        gives = []
        for dx, dz in far:
            k = chip_at(dx, dz)
            gives.append(
                remote(
                    part.at[t, rows_of(k), :],
                    parts.at[t, chip],
                    rs_send.at[t, dx * Z + dz],
                    rs_recv.at[t, chip],
                    prev,
                    dev(k, core),
                )
            )
            gives[-1].start()
        if t == 0 or last:
            for c in range(2):
                remote(
                    own.at[:, :, pl.ds(c * HALF, HALF)],
                    state.at[t, :, pl.ds(c * 8, 8), :],
                    st_send.at[t, c],
                    st_recv.at[t, c],
                    s,
                    me,
                ).wait_recv()
        else:
            remote(
                fresh.at[t], state.at[t], st_send.at[t, 0], st_recv.at[t, 0], s, me
            ).wait_recv()
        for dx, dz in far[::-1]:
            k = chip_at(dx, dz)
            remote(
                part.at[t, rows_of(k), :], parts.at[t, k], rs_send.at[t, 0], rs_recv.at[t, k], s, me
            ).wait_recv()
        grads = jnp.sum(parts[t].astype(jnp.float32), axis=0)
        momentum = inertia * state[t, 1] + FACTOR * grads
        items = state[t, 0] - item_rate * momentum
        if last:
            for h in range(2):
                items_out[:, h * HALF : h * HALF + HALF] = items[h * 8 : h * 8 + 8]
                momentum_out[:, h * HALF : h * HALF + HALF] = momentum[h * 8 : h * 8 + 8]
        else:
            w[t + 1, core, rows_of(chip), :] = items.astype(jnp.bfloat16)

            def place(c, k, t=t + 1):
                return w.at[t, c, rows_of(k), :]

            sends, passed, pass_on = spread(t + 1, place)
            fresh[t, 0] = items
            fresh[t, 1] = momentum
            if t == STEPS - 2:
                for c in range(2):
                    moves.append(
                        remote(
                            fresh.at[t, :, pl.ds(c * 8, 8), :],
                            state.at[t + 1, :, pl.ds(pl.multiple_of(core * 8, 8), 8), :],
                            st_send.at[t + 1, c],
                            st_recv.at[t + 1, core],
                            prev,
                            dev(chip, c),
                        )
                    )
                    moves[-1].start()
            else:
                moves.append(
                    remote(
                        fresh.at[t],
                        state.at[t + 1],
                        st_send.at[t + 1, 0],
                        st_recv.at[t + 1, 0],
                        prev,
                        me,
                    )
                )
                moves[-1].start()
            collect(t + 1, place, pass_on)
        moves += [*gives, swap]
    finish(moves)
    for copy in store:
        copy.wait()


def local(users, items, momentum, ratings):
    bf16, f32 = jnp.bfloat16, jnp.float32
    any_space = pl.BlockSpec(memory_space=pl.ANY)
    vmem = pl.BlockSpec(memory_space=pltpu.VMEM)
    dma = pltpu.SemaphoreType.DMA
    return pl.pallas_call(
        kernel,
        out_shape=(
            jax.ShapeDtypeStruct(users.shape, bf16),
            jax.ShapeDtypeStruct(items.shape, f32),
            jax.ShapeDtypeStruct(items.shape, f32),
        ),
        in_specs=[any_space] * 4,
        out_specs=(any_space, vmem, vmem),
        scratch_shapes=[
            pltpu.VMEM((2, USERS, HALF), bf16),
            pltpu.VMEM((USERS, STEPS, BLOCK), bf16),
            pltpu.VMEM((STEPS, USERS, BLOCK), bf16),
            pltpu.VMEM((128 * STEPS, 128), f32),
            pltpu.VMEM((128 * STEPS, 128), f32),
            pltpu.VMEM((2, 8, R), f32),
            pltpu.VMEM((2, CHIPS, ROWS, HALF), bf16),
            pltpu.VMEM((STEPS, 2, BLOCK, HALF), bf16),
            pltpu.VMEM((USERS, BLOCK), f32),
            pltpu.VMEM((USERS, BLOCK), bf16),
            pltpu.VMEM((BLOCK, USERS), bf16),
            pltpu.VMEM((2, CHIPS, 2, 8, HALF), f32),
            pltpu.VMEM((STEPS, BLOCK, HALF), bf16),
            pltpu.VMEM((STEPS, BLOCK, HALF), bf16),
            pltpu.VMEM((STEPS, BLOCK, HALF), bf16),
            pltpu.VMEM((STEPS, CHIPS, ROWS, HALF), bf16),
            pltpu.VMEM((STEPS, 2, ROWS, HALF), f32),
            pltpu.VMEM((STEPS, 2, ROWS, HALF), f32),
            dma((5,)),
            dma((STEPS, CHIPS)),
            dma((STEPS, CHIPS)),
            dma((STEPS, CHIPS)),
            dma((STEPS, CHIPS)),
            dma((STEPS,)),
            dma((STEPS,)),
            dma((STEPS, CHIPS)),
            dma((STEPS, CHIPS)),
            dma((STEPS, 2)),
            dma((STEPS, 2)),
        ],
        compiler_params=pltpu.CompilerParams(
            collective_id=0, has_side_effects=True, vmem_limit_bytes=62 * 1024 * 1024
        ),
        cost_estimate=pl.CostEstimate(
            flops=STEPS * 6 * USERS * BLOCK * R,
            bytes_accessed=4 * 1024 * 1024,
            transcendentals=0,
        ),
    )(users, items, momentum, ratings)


def solution(mesh):
    rows = P(("stratum", "user"), None)
    return jax.shard_map(
        local,
        mesh=mesh,
        in_specs=(rows, rows, rows, P(("stratum", "user"), None, None)),
        out_specs=(rows, rows, rows),
        check_vma=False,
    )
```

time: 225 us -> 97.4 us (0.43)
  starting transfers between devices: 109 us -> 0 us
  Pallas kernels: 0 us -> 92.8 us
  waiting for transfers between devices: 65.5 us -> 0 us
  blocking collectives: 22 us -> 0 us
  matrix products: 12.5 us -> 0 us
  local copies, waits for them, and re-layouts: 13.1 us -> 3.49 us
    pallas_call x0 -> x1, Pallas kernels: none -> 92.8 us  [local(): pl.pallas_call(kernel, out_shape=(jax.ShapeDtypeStruct(users.shape, bf16)...]
    ppermute x8 -> x0, starting transfers between devices: 72.5 us -> none  [shifted(): return lax.ppermute(block, axis, route)]
    all_to_all x7 -> x0, waiting for transfers between devices: 58 us -> none  [the longest x4 35.2 us: copy_for_each(): lax.all_to_all(jnp.broadcast_to(x[None], (size, *x.shape)), axis, 0, 0, t...]
    all_to_all x7 -> x0, starting transfers between devices: 36 us -> none  [the longest x4 25 us: copy_for_each(): lax.all_to_all(jnp.broadcast_to(x[None], (size, *x.shape)), axis, 0, 0, t...]
    all_to_all x1 -> x0, blocking collectives: 22 us -> none  [summed_on_arrival(): tiles = lax.all_to_all(cut_along(x, dim, size), axis, 0, 0, tiled=True)]
    dot_general x12 -> x0, matrix products: 12.5 us -> none  [the longest x4 5.54 us: local(): lax.dot_general(users, whole, (((1,), (1,)), ((), ())), preferred_element...]
    slice x1 -> x0, local copies, waits for them, and re-layouts: 8.92 us -> none  [local(): tile = ratings[:, step, :]]
    ppermute x8 -> x0, waiting for transfers between devices: 7.54 us -> none  [shifted(): return lax.ppermute(block, axis, route)]
  transfers between devices with their start and end apart: 15 -> 0, of which waited for: 11 -> 0; matrix products, arithmetic and copies ran while one was open for 5% -> 0% of each run, Pallas kernels for 0% -> 0%
where the time goes in v1:
time: 97.4 us; the launch traced here: 96.9 us
  Pallas kernels  92.8 us (95%)
  local copies, waits for them, and re-layouts  3.49 us (4%)
    pallas_call x1, Pallas kernels, local(): pl.pallas_call(kernel, out_shape=(jax.ShapeDtypeStruct(users.shape, bf16)...  92.8 us
    unnamed x7, local copies, waits for them, and re-layouts  3.49 us

profile of v1, /device:TPU:1, one launch (start us, length us, event | category | flops | bytes accessed | tf_op | source)
XLA Modules:
  0.0 96.9 jit_solution(6673764375735703076)
XLA Ops:
  0.6 92.8 %shard_map.67 = (bf16[1024,512]{1,0:T(8,128)(2,1)}, f32[8,512]{1,0:T(8,128)}, f32[8,512]{1,0:T(8,128)}) custom-call(bf16[1024,512]{1,0:T(8,128)(2,1)} %users_in.1, f32[8,512]{1,0:T(8,128)} %items_in.1, f32[8,512]{1,0:T(8,128)} %momentum_in.1, bf16[1024,4,256]{2,1,0:T(4,128)(2,1)} %ratings_in.1), custom_call_target="tpu_custom_call" | custom-call | flops 3221225472 | bytes 4194304 | tf_op jit(solution)/shard_map/pallas_call | solution.py:359
  93.4 0.0 copy-start.1
  93.4 0.0 copy-start
  93.4 2.3 %copy.10 = bf16[1024,512]{1,0:T(8,128)(2,1)} copy(bf16[1024,512]{1,0:T(8,128)(2,1)} %get-tuple-element.6) | data formatting | bytes 2097152
  95.7 0.0 copy-done.1
  95.7 0.6 copy.11
  96.3 0.0 copy-done
  96.3 0.6 copy.12
Async XLA Ops:
  93.4 2.3 %copy-start.1 = (f32[8,512]{1,0:T(8,128)S(1)}, f32[8,512]{1,0:T(8,128)}, u32[]{:S(2)}) copy-start(f32[8,512]{1,0:T(8,128)} %get-tuple-element.7) | copy-start | bytes 49156
  93.4 2.9 %copy-start = (f32[8,512]{1,0:T(8,128)S(1)}, f32[8,512]{1,0:T(8,128)}, u32[]{:S(2)}) copy-start(f32[8,512]{1,0:T(8,128)} %get-tuple-element.8) | copy-start | bytes 49156

commit v2 on v1

--- a/solution.py
+++ b/solution.py
@@ -96,26 +96,22 @@
         copy.start()
 
     far = [(dx, dz) for dx in (2, 1, 3, 0) for dz in (2, 1, 3, 0)]
+    far_prev = [(dx, dz) for dx in (2, 1, 3, 0) for dz in (0, 1, 3, 2)]
     barrier = pltpu.get_barrier_semaphore()
 
     def hello(stratum, user):
         pl.semaphore_signal(barrier, inc=1, device_id=(stratum, user), device_id_type=MESH)
 
-    for dx, dz in far:
-        k = chip_at(dx, dz)
-        hello(prev, dev(k, core))
-        hello(nxt, dev(k, core))
-        if (dx, dz) != (0, 0):
-            hello(s, dev(k, core))
-    hello(prev, dev(chip, other))
-    hello(nxt, dev(chip, other))
+    for dx, dz in far[:-1]:
+        hello(s, dev(chip_at(dx, dz), core))
+    hello(nxt, me)
     hello(s, dev(chip, other))
     loads[0].wait()
     loads[1].wait()
     first[core, chip] = jnp.concatenate([own[0, :, :HALF], own[0, :, HALF:]], axis=0).astype(
         jnp.bfloat16
     )
-    pl.semaphore_wait(barrier, 3 * CHIPS + 2)
+    pl.semaphore_wait(barrier, CHIPS + 1)
 
     def remote(src, dst, send, recv, stratum, user):
         return pltpu.make_async_remote_copy(
@@ -172,20 +168,6 @@
         return first.at[c, k]
 
     sends, passed, pass_on = spread(0, place_first)
-    moves = []
-    for c in range(2):
-        moves.append(
-            remote(
-                own.at[:, :, pl.ds(c * HALF, HALF)],
-                state.at[0, :, pl.ds(pl.multiple_of(core * 8, 8), 8), :],
-                st_send.at[0, c],
-                st_recv.at[0, core],
-                prev,
-                dev(chip, c),
-            )
-        )
-        moves[-1].start()
-
     loads[2].wait()
 
     def split(i, _):
@@ -214,7 +196,28 @@
             .astype(jnp.bfloat16)
         )
 
-    store = []
+    moves = []
+
+    def pass_state(src, t, split_rows):
+        if not split_rows:
+            moves.append(
+                remote(src, state.at[t], st_send.at[t, 0], st_recv.at[t, 0], prev, me)
+            )
+            moves[-1].start()
+            return
+        for c in range(2):
+            moves.append(
+                remote(
+                    src.at[:, :, pl.ds(c * HALF, HALF)] if t == 0 else src.at[:, pl.ds(c * 8, 8), :],
+                    state.at[t, :, pl.ds(pl.multiple_of(core * 8, 8), 8), :],
+                    st_send.at[t, c],
+                    st_recv.at[t, core],
+                    prev,
+                    dev(chip, c),
+                )
+            )
+            moves[-1].start()
+
     for t in range(STEPS):
         last = t == STEPS - 1
 
@@ -223,12 +226,14 @@
 
         tiles = [pl.ds(i * TILE, TILE) for i in range(USERS // TILE)]
         if t == 0:
+            pass_state(own, 0, True)
             for r in tiles:
                 score[r, :] = dot(u[core, r, :], w[t, core], NT)
         else:
             for r in tiles:
                 score[r, :] = dot(u[core, r, :], w[t, core], NT)
             collect_passed(t, place)
+            pass_state(fresh.at[t - 1], t, last)
             finish(sends + passed)
         for r in tiles:
             total = score[r, :] + dot(u[other, r, :], w[t, other], NT)
@@ -256,22 +261,18 @@
         for h in range(2):
             for r in tiles:
                 change = dot(e[r, :], w[t, h], NN)
-                u[h, r, :] = (
-                    u[h, r, :].astype(jnp.float32) - user_rate * FACTOR * change
-                ).astype(jnp.bfloat16)
-        if last:
-            for h in range(2):
-                store.append(
-                    pltpu.make_async_copy(
-                        u.at[h], users_out.at[:, pl.ds(h * HALF, HALF)], load_sem.at[3 + h]
-                    )
+                moved = (u[h, r, :].astype(jnp.float32) - user_rate * FACTOR * change).astype(
+                    jnp.bfloat16
                 )
-                store[-1].start()
+                if last:
+                    users_out[r, h * HALF : h * HALF + HALF] = moved
+                else:
+                    u[h, r, :] = moved
         swap.wait_recv()
         mine = piece_for(core) if last else g[0].reshape(BLOCK, HALF)
         part[t] = (mine + take[t].astype(jnp.float32)).astype(jnp.bfloat16)
         gives = []
-        for dx, dz in far:
+        for dx, dz in far_prev:
             k = chip_at(dx, dz)
             gives.append(
                 remote(
@@ -298,7 +299,7 @@
             remote(
                 fresh.at[t], state.at[t], st_send.at[t, 0], st_recv.at[t, 0], s, me
             ).wait_recv()
-        for dx, dz in far[::-1]:
+        for dx, dz in far_prev[::-1]:
             k = chip_at(dx, dz)
             remote(
                 part.at[t, rows_of(k), :], parts.at[t, k], rs_send.at[t, 0], rs_recv.at[t, k], s, me
@@ -319,35 +320,20 @@
             sends, passed, pass_on = spread(t + 1, place)
             fresh[t, 0] = items
             fresh[t, 1] = momentum
-            if t == STEPS - 2:
-                for c in range(2):
-                    moves.append(
-                        remote(
-                            fresh.at[t, :, pl.ds(c * 8, 8), :],
-                            state.at[t + 1, :, pl.ds(pl.multiple_of(core * 8, 8), 8), :],
-                            st_send.at[t + 1, c],
-                            st_recv.at[t + 1, core],
-                            prev,
-                            dev(chip, c),
-                        )
-                    )
-                    moves[-1].start()
-            else:
-                moves.append(
-                    remote(
-                        fresh.at[t],
-                        state.at[t + 1],
-                        st_send.at[t + 1, 0],
-                        st_recv.at[t + 1, 0],
-                        prev,
-                        me,
-                    )
-                )
-                moves[-1].start()
             collect(t + 1, place, pass_on)
         moves += [*gives, swap]
     finish(moves)
-    for copy in store:
+
+
+def write_out(users, items, momentum, users_out, items_out, momentum_out, sem):
+    copies = [
+        pltpu.make_async_copy(users, users_out, sem.at[0]),
+        pltpu.make_async_copy(items, items_out, sem.at[1]),
+        pltpu.make_async_copy(momentum, momentum_out, sem.at[2]),
+    ]
+    for copy in copies:
+        copy.start()
+    for copy in copies:
         copy.wait()
 
 
@@ -356,15 +342,18 @@
     any_space = pl.BlockSpec(memory_space=pl.ANY)
     vmem = pl.BlockSpec(memory_space=pltpu.VMEM)
     dma = pltpu.SemaphoreType.DMA
-    return pl.pallas_call(
+    inputs = [
+        pltpu.with_memory_space_constraint(a, pltpu.HBM) for a in (users, items, momentum, ratings)
+    ]
+    outs = pl.pallas_call(
         kernel,
         out_shape=(
-            jax.ShapeDtypeStruct(users.shape, bf16),
-            jax.ShapeDtypeStruct(items.shape, f32),
-            jax.ShapeDtypeStruct(items.shape, f32),
+            pltpu.VMEM(users.shape, bf16),
+            pltpu.VMEM(items.shape, f32),
+            pltpu.VMEM(items.shape, f32),
         ),
         in_specs=[any_space] * 4,
-        out_specs=(any_space, vmem, vmem),
+        out_specs=(vmem, vmem, vmem),
         scratch_shapes=[
             pltpu.VMEM((2, USERS, HALF), bf16),
             pltpu.VMEM((USERS, STEPS, BLOCK), bf16),
@@ -397,14 +386,26 @@
             dma((STEPS, 2)),
         ],
         compiler_params=pltpu.CompilerParams(
-            collective_id=0, has_side_effects=True, vmem_limit_bytes=62 * 1024 * 1024
+            collective_id=0, has_side_effects=True, vmem_limit_bytes=48 * 1024 * 1024
         ),
         cost_estimate=pl.CostEstimate(
             flops=STEPS * 6 * USERS * BLOCK * R,
             bytes_accessed=4 * 1024 * 1024,
             transcendentals=0,
         ),
-    )(users, items, momentum, ratings)
+    )(*inputs)
+    outs = [pltpu.with_memory_space_constraint(a, pltpu.VMEM) for a in outs]
+    return pl.pallas_call(
+        write_out,
+        out_shape=(
+            jax.ShapeDtypeStruct(users.shape, bf16),
+            jax.ShapeDtypeStruct(items.shape, f32),
+            jax.ShapeDtypeStruct(items.shape, f32),
+        ),
+        in_specs=[any_space] * 3,
+        out_specs=(any_space,) * 3,
+        scratch_shapes=[dma((3,))],
+    )(*outs)
 
 
 def solution(mesh):

time: 97.4 us -> 89.9 us (0.923)
  Pallas kernels: 92.8 us -> 88.3 us
  local copies, waits for them, and re-layouts: 3.49 us -> 0 us
    pallas_call x1 -> x2, Pallas kernels: 92.8 us -> 88.3 us  [the longest x1 87.3 us: local(): pl.pallas_call(kernel, out_shape=(pltpu.VMEM(users.shape, bf16), pltpu.VM...]
    unnamed x7 -> x0, local copies, waits for them, and re-layouts: 3.49 us -> none
where the time goes in v2:
time: 89.9 us; the launch traced here: 89 us
  Pallas kernels  88.3 us (98%)
    pallas_call x1, Pallas kernels, local(): pl.pallas_call(kernel, out_shape=(pltpu.VMEM(users.shape, bf16), pltpu.VM...  87.3 us

profile of v2, /device:TPU:1, one launch (start us, length us, event | category | flops | bytes accessed | tf_op | source)
XLA Modules:
  0.0 89.0 jit_solution(14722772761010477430)
XLA Ops:
  0.6 87.3 %shard_map.67 = (bf16[1024,512]{1,0:T(8,128)(2,1)S(1)}, f32[8,512]{1,0:T(8,128)S(1)}, f32[8,512]{1,0:T(8,128)S(1)}) custom-call(bf16[1024,512]{1,0:T(8,128)(2,1)} %users_in.1, f32[8,512]{1,0:T(8,128)} %items_in.1, f32[8,512]{1,0:T(8,128)} %momentum_in.1, bf16[1024,4,256]{2,1,0:T(4,128)(2,1)} %ratings_in.1), custom_call_target="tpu_custom_call" | custom-call | flops 3221225472 | bytes 4194304 | tf_op jit(solution)/shard_map/pallas_call | solution.py:348
  88.0 1.0 %shard_map.68 = (bf16[1024,512]{1,0:T(8,128)(2,1)}, f32[8,512]{1,0:T(8,128)}, f32[8,512]{1,0:T(8,128)}) custom-call(bf16[1024,512]{1,0:T(8,128)(2,1)S(1)} %get-tuple-element.6.users, f32[8,512]{1,0:T(8,128)S(1)} %get-tuple-element.7.items, f32[8,512]{1,0:T(8,128)S(1)} %get-tuple-element.8.momentum), custom_call_target="tpu_custom_call" | custom-call | tf_op jit(solution)/shard_map/pallas_call | solution.py:398

commit v3 on v2

--- a/solution.py
+++ b/solution.py
@@ -55,6 +55,8 @@
     give,
     take,
     part,
+    along_x,
+    line,
     parts,
     state,
     fresh,
@@ -65,6 +67,8 @@
     fw_recv,
     sib_send,
     sib_recv,
+    x_send,
+    x_recv,
     rs_send,
     rs_recv,
     st_send,
@@ -92,20 +96,19 @@
         pltpu.make_async_copy(users_in.at[:, pl.ds(0, HALF)], u.at[0], load_sem.at[3]),
         pltpu.make_async_copy(users_in.at[:, pl.ds(HALF, HALF)], u.at[1], load_sem.at[4]),
     ]
+
+    far = [(dx, dz) for dx in (2, 1, 3, 0) for dz in (2, 1, 3, 0)]
+    barrier = pltpu.get_barrier_semaphore()
+
+    def hello(stratum, user):
+        pl.semaphore_signal(barrier, inc=1, device_id=(stratum, user), device_id_type=MESH)
+
+    hello(nxt, me)
+    for dx, dz in far[:-1]:
+        hello(s, dev(chip_at(dx, dz), core))
+    hello(s, dev(chip, other))
     for copy in loads:
         copy.start()
-
-    far = [(dx, dz) for dx in (2, 1, 3, 0) for dz in (2, 1, 3, 0)]
-    far_prev = [(dx, dz) for dx in (2, 1, 3, 0) for dz in (0, 1, 3, 2)]
-    barrier = pltpu.get_barrier_semaphore()
-
-    def hello(stratum, user):
-        pl.semaphore_signal(barrier, inc=1, device_id=(stratum, user), device_id_type=MESH)
-
-    for dx, dz in far[:-1]:
-        hello(s, dev(chip_at(dx, dz), core))
-    hello(nxt, me)
-    hello(s, dev(chip, other))
     loads[0].wait()
     loads[1].wait()
     first[core, chip] = jnp.concatenate([own[0, :, :HALF], own[0, :, HALF:]], axis=0).astype(
@@ -122,6 +125,9 @@
             device_id=(stratum, user),
             device_id_type=MESH,
         )
+
+    def lines_of(k):
+        return pl.ds(pl.multiple_of(k * (Z * ROWS), Z * ROWS), Z * ROWS)
 
     def rows_of(k):
         return pl.ds(pl.multiple_of(k * ROWS, ROWS), ROWS)
@@ -272,16 +278,34 @@
         mine = piece_for(core) if last else g[0].reshape(BLOCK, HALF)
         part[t] = (mine + take[t].astype(jnp.float32)).astype(jnp.bfloat16)
         gives = []
-        for dx, dz in far_prev:
-            k = chip_at(dx, dz)
+        for dx in (2, 1, 3):
+            x_of = (mx + dx) % X
             gives.append(
                 remote(
-                    part.at[t, rows_of(k), :],
-                    parts.at[t, chip],
-                    rs_send.at[t, dx * Z + dz],
-                    rs_recv.at[t, chip],
+                    part.at[t, lines_of(x_of), :],
+                    along_x.at[t, dx - 1],
+                    x_send.at[t, dx - 1],
+                    x_recv.at[t, dx - 1],
+                    s,
+                    dev(x_of * Z + mz, core),
+                )
+            )
+            gives[-1].start()
+        total = part[t, lines_of(mx), :].astype(jnp.float32)
+        for i in (1, 2, 0):
+            gives[(2, 1, 3).index(i + 1)].wait_recv()
+            total += along_x[t, i].astype(jnp.float32)
+        line[t] = total.astype(jnp.bfloat16)
+        for dz in (0, 1, 3, 2):
+            z_of = (mz + dz) % Z
+            gives.append(
+                remote(
+                    line.at[t, rows_of(z_of), :],
+                    parts.at[t, mz],
+                    rs_send.at[t, dz],
+                    rs_recv.at[t, mz],
                     prev,
-                    dev(k, core),
+                    dev(mx * Z + z_of, core),
                 )
             )
             gives[-1].start()
@@ -299,10 +323,14 @@
             remote(
                 fresh.at[t], state.at[t], st_send.at[t, 0], st_recv.at[t, 0], s, me
             ).wait_recv()
-        for dx, dz in far_prev[::-1]:
-            k = chip_at(dx, dz)
+        for z_of in range(Z):
             remote(
-                part.at[t, rows_of(k), :], parts.at[t, k], rs_send.at[t, 0], rs_recv.at[t, k], s, me
+                line.at[t, rows_of(0), :],
+                parts.at[t, z_of],
+                rs_send.at[t, 0],
+                rs_recv.at[t, z_of],
+                s,
+                me,
             ).wait_recv()
         grads = jnp.sum(parts[t].astype(jnp.float32), axis=0)
         momentum = inertia * state[t, 1] + FACTOR * grads
@@ -370,7 +398,9 @@
             pltpu.VMEM((STEPS, BLOCK, HALF), bf16),
             pltpu.VMEM((STEPS, BLOCK, HALF), bf16),
             pltpu.VMEM((STEPS, BLOCK, HALF), bf16),
-            pltpu.VMEM((STEPS, CHIPS, ROWS, HALF), bf16),
+            pltpu.VMEM((STEPS, X - 1, Z * ROWS, HALF), bf16),
+            pltpu.VMEM((STEPS, Z * ROWS, HALF), bf16),
+            pltpu.VMEM((STEPS, Z, ROWS, HALF), bf16),
             pltpu.VMEM((STEPS, 2, ROWS, HALF), f32),
             pltpu.VMEM((STEPS, 2, ROWS, HALF), f32),
             dma((5,)),
@@ -380,8 +410,10 @@
             dma((STEPS, CHIPS)),
             dma((STEPS,)),
             dma((STEPS,)),
-            dma((STEPS, CHIPS)),
-            dma((STEPS, CHIPS)),
+            dma((STEPS, X - 1)),
+            dma((STEPS, X - 1)),
+            dma((STEPS, Z)),
+            dma((STEPS, Z)),
             dma((STEPS, 2)),
             dma((STEPS, 2)),
         ],

time: 89.9 us -> 86.1 us (0.958)
  Pallas kernels: 88.3 us -> 83.8 us
    pallas_call x1, Pallas kernels: 87.3 us -> 82.8 us  [local(): pl.pallas_call(kernel, out_shape=(pltpu.VMEM(users.shape, bf16), pltpu.VM...]
where the time goes in v3:
time: 86.1 us; the launch traced here: 84.4 us
  Pallas kernels  83.8 us (97%)
    pallas_call x1, Pallas kernels, local(): pl.pallas_call(kernel, out_shape=(pltpu.VMEM(users.shape, bf16), pltpu.VM...  82.8 us

profile of v3, /device:TPU:1, one launch (start us, length us, event | category | flops | bytes accessed | tf_op | source)
XLA Modules:
  0.0 84.4 jit_solution(13473184278415401776)
XLA Ops:
  0.6 82.8 %shard_map.67 = (bf16[1024,512]{1,0:T(8,128)(2,1)S(1)}, f32[8,512]{1,0:T(8,128)S(1)}, f32[8,512]{1,0:T(8,128)S(1)}) custom-call(bf16[1024,512]{1,0:T(8,128)(2,1)} %users_in.1, f32[8,512]{1,0:T(8,128)} %items_in.1, f32[8,512]{1,0:T(8,128)} %momentum_in.1, bf16[1024,4,256]{2,1,0:T(4,128)(2,1)} %ratings_in.1), custom_call_target="tpu_custom_call" | custom-call | flops 3221225472 | bytes 4194304 | tf_op jit(solution)/shard_map/pallas_call | solution.py:376
  83.4 1.0 %shard_map.68 = (bf16[1024,512]{1,0:T(8,128)(2,1)}, f32[8,512]{1,0:T(8,128)}, f32[8,512]{1,0:T(8,128)}) custom-call(bf16[1024,512]{1,0:T(8,128)(2,1)S(1)} %get-tuple-element.6.users, f32[8,512]{1,0:T(8,128)S(1)} %get-tuple-element.7.items, f32[8,512]{1,0:T(8,128)S(1)} %get-tuple-element.8.momentum), custom_call_target="tpu_custom_call" | custom-call | tf_op jit(solution)/shard_map/pallas_call | solution.py:430

commit v4 on v3

--- a/solution.py
+++ b/solution.py
@@ -97,6 +97,8 @@
         pltpu.make_async_copy(users_in.at[:, pl.ds(HALF, HALF)], u.at[1], load_sem.at[4]),
     ]
 
+    loads[0].start()
+    loads[1].start()
     far = [(dx, dz) for dx in (2, 1, 3, 0) for dz in (2, 1, 3, 0)]
     barrier = pltpu.get_barrier_semaphore()
 
@@ -107,7 +109,7 @@
     for dx, dz in far[:-1]:
         hello(s, dev(chip_at(dx, dz), core))
     hello(s, dev(chip, other))
-    for copy in loads:
+    for copy in loads[2:]:
         copy.start()
     loads[0].wait()
     loads[1].wait()
@@ -258,10 +260,18 @@
             give[t] = piece_for(other).astype(jnp.bfloat16)
         else:
             give[t] = dot(et[...], u[other], NN).astype(jnp.bfloat16)
-        swap = remote(
-            give.at[t], take.at[t], sib_send.at[t], sib_recv.at[t], s, dev(chip, other)
-        )
-        swap.start()
+        swaps = {}
+        for dx in (2, 1, 3, 0):
+            lines = lines_of((mx + dx) % X)
+            swaps[dx] = remote(
+                give.at[t, lines, :],
+                take.at[t, lines, :],
+                sib_send.at[t, dx],
+                sib_recv.at[t, dx],
+                s,
+                dev(chip, other),
+            )
+            swaps[dx].start()
         if not last:
             g[0] = dot(et[...], u[core], NN).reshape(CHIPS, 2, 8, HALF)
         for h in range(2):
@@ -274,12 +284,22 @@
                     users_out[r, h * HALF : h * HALF + HALF] = moved
                 else:
                     u[h, r, :] = moved
-        swap.wait_recv()
-        mine = piece_for(core) if last else g[0].reshape(BLOCK, HALF)
-        part[t] = (mine + take[t].astype(jnp.float32)).astype(jnp.bfloat16)
+
+        def chip_sum(dx, t=t, last=last, swaps=swaps):
+            x_of = (mx + dx) % X
+            four = pl.ds(x_of * Z, Z)
+            if last:
+                both = [g[h, four, pl.ds(core, 1)] for h in range(2)]
+                mine = jnp.concatenate(both, axis=1)
+            else:
+                mine = g[0, four]
+            swaps[dx].wait_recv()
+            return mine.reshape(Z * ROWS, HALF) + take[t, lines_of(x_of), :].astype(jnp.float32)
+
         gives = []
         for dx in (2, 1, 3):
             x_of = (mx + dx) % X
+            part[t, lines_of(x_of), :] = chip_sum(dx).astype(jnp.bfloat16)
             gives.append(
                 remote(
                     part.at[t, lines_of(x_of), :],
@@ -291,7 +311,7 @@
                 )
             )
             gives[-1].start()
-        total = part[t, lines_of(mx), :].astype(jnp.float32)
+        total = chip_sum(0)
         for i in (1, 2, 0):
             gives[(2, 1, 3).index(i + 1)].wait_recv()
             total += along_x[t, i].astype(jnp.float32)
@@ -349,7 +369,7 @@
             fresh[t, 0] = items
             fresh[t, 1] = momentum
             collect(t + 1, place, pass_on)
-        moves += [*gives, swap]
+        moves += [*gives, *swaps.values()]
     finish(moves)
 
 
@@ -408,8 +428,8 @@
             dma((STEPS, CHIPS)),
             dma((STEPS, CHIPS)),
             dma((STEPS, CHIPS)),
-            dma((STEPS,)),
-            dma((STEPS,)),
+            dma((STEPS, X)),
+            dma((STEPS, X)),
             dma((STEPS, X - 1)),
             dma((STEPS, X - 1)),
             dma((STEPS, Z)),

time: 86.1 us -> 85.7 us (level)
  no operation moved by 1% of the time
where the time goes in v4:
time: 85.7 us; the launch traced here: 84.1 us
  Pallas kernels  83.4 us (97%)
    pallas_call x1, Pallas kernels, local(): pl.pallas_call(kernel, out_shape=(pltpu.VMEM(users.shape, bf16), pltpu.VM...  82.4 us

profile of v4, /device:TPU:1, one launch (start us, length us, event | category | flops | bytes accessed | tf_op | source)
XLA Modules:
  0.0 84.1 jit_solution(4515023484165423210)
XLA Ops:
  0.6 82.4 %shard_map.67 = (bf16[1024,512]{1,0:T(8,128)(2,1)S(1)}, f32[8,512]{1,0:T(8,128)S(1)}, f32[8,512]{1,0:T(8,128)S(1)}) custom-call(bf16[1024,512]{1,0:T(8,128)(2,1)} %users_in.1, f32[8,512]{1,0:T(8,128)} %items_in.1, f32[8,512]{1,0:T(8,128)} %momentum_in.1, bf16[1024,4,256]{2,1,0:T(4,128)(2,1)} %ratings_in.1), custom_call_target="tpu_custom_call" | custom-call | flops 3221225472 | bytes 4194304 | tf_op jit(solution)/shard_map/pallas_call | solution.py:396
  83.1 1.0 %shard_map.68 = (bf16[1024,512]{1,0:T(8,128)(2,1)}, f32[8,512]{1,0:T(8,128)}, f32[8,512]{1,0:T(8,128)}) custom-call(bf16[1024,512]{1,0:T(8,128)(2,1)S(1)} %get-tuple-element.6.users, f32[8,512]{1,0:T(8,128)S(1)} %get-tuple-element.7.items, f32[8,512]{1,0:T(8,128)S(1)} %get-tuple-element.8.momentum), custom_call_target="tpu_custom_call" | custom-call | tf_op jit(solution)/shard_map/pallas_call | solution.py:450

commit v5 on v4

--- a/solution.py
+++ b/solution.py
@@ -89,6 +89,7 @@
     def dev(k, c):
         return k * 2 + c
 
+    middle = (mz - 1) * (mz - 2) == 0
     loads = [
         pltpu.make_async_copy(items_in, own.at[0], load_sem.at[0]),
         pltpu.make_async_copy(momentum_in, own.at[1], load_sem.at[1]),
@@ -97,8 +98,6 @@
         pltpu.make_async_copy(users_in.at[:, pl.ds(HALF, HALF)], u.at[1], load_sem.at[4]),
     ]
 
-    loads[0].start()
-    loads[1].start()
     far = [(dx, dz) for dx in (2, 1, 3, 0) for dz in (2, 1, 3, 0)]
     barrier = pltpu.get_barrier_semaphore()
 
@@ -109,7 +108,7 @@
     for dx, dz in far[:-1]:
         hello(s, dev(chip_at(dx, dz), core))
     hello(s, dev(chip, other))
-    for copy in loads[2:]:
+    for copy in loads:
         copy.start()
     loads[0].wait()
     loads[1].wait()
@@ -134,33 +133,30 @@
     def rows_of(k):
         return pl.ds(pl.multiple_of(k * ROWS, ROWS), ROWS)
 
-    def spread(t, place):
+    def finish(sends):
+        for copy in sends:
+            copy.wait_send()
+
+    def pass_on(t, place, k):
+        piece = place(core, k)
+        copy = remote(piece, piece, fw_send.at[t, k], fw_recv.at[t, k], s, dev(chip, other))
+        copy.start()
+        return copy
+
+    def spread(t, q, place, k):
+        mine = place(core, k)
         sends = []
-        mine = place(core, chip)
         for dx, dz in far[:-1]:
-            k = chip_at(dx, dz)
+            to = dev(chip_at(dx, dz), core)
             sends.append(
-                remote(mine, mine, ag_send.at[t, dx * Z + dz], ag_recv.at[t, chip], s, dev(k, core))
+                remote(mine, mine, ag_send.at[t, q, dx * Z + dz], ag_recv.at[t, k], s, to)
             )
             sends[-1].start()
-        passed = []
-
-        def pass_on(k, slot):
-            piece = place(core, k)
-            passed.append(
-                remote(piece, piece, fw_send.at[t, slot], fw_recv.at[t, k], s, dev(chip, other))
-            )
-            passed[-1].start()
-
-        pass_on(chip, 0)
-        return sends, passed, pass_on
-
-    def collect(t, place, pass_on):
-        for slot, (dx, dz) in enumerate(far[:-1][::-1]):
-            k = chip_at(dx, dz)
-            piece = place(core, k)
-            remote(piece, piece, ag_send.at[t, 0], ag_recv.at[t, k], s, me).wait_recv()
-            pass_on(k, slot + 1)
+        return sends
+
+    def arrived(t, place, k):
+        piece = place(core, k)
+        remote(piece, piece, ag_send.at[t, 0, 0], ag_recv.at[t, k], s, me).wait_recv()
 
     def collect_passed(t, place):
         for dx, dz in far[::-1]:
@@ -168,14 +164,17 @@
             piece = place(other, k)
             remote(piece, piece, fw_send.at[t, 0], fw_recv.at[t, k], s, me).wait_recv()
 
-    def finish(sends):
-        for copy in sends:
-            copy.wait_send()
+    def finish_passed(t, place):
+        for k in range(CHIPS):
+            piece = place(core, k)
+            remote(piece, piece, fw_send.at[t, k], fw_recv.at[t, 0], s, me).wait_send()
 
     def place_first(c, k):
         return first.at[c, k]
 
-    sends, passed, pass_on = spread(0, place_first)
+    sends = spread(0, 0, place_first, chip)
+    pass_on(0, place_first, chip)
+
     loads[2].wait()
 
     def split(i, _):
@@ -193,9 +192,13 @@
     loads[3].wait()
     loads[4].wait()
 
-    collect(0, place_first, pass_on)
+    for dx, dz in far[:-1][::-1]:
+        k = chip_at(dx, dz)
+        arrived(0, place_first, k)
+        pass_on(0, place_first, k)
     collect_passed(0, place_first)
-    finish(sends + passed)
+    finish(sends)
+    finish_passed(0, place_first)
     pieces = [first[c].astype(jnp.float32).reshape(CHIPS, 2, 8, HALF) for c in range(2)]
     for h in range(2):
         w[0, h] = (
@@ -204,27 +207,80 @@
             .astype(jnp.bfloat16)
         )
 
-    moves = []
-
-    def pass_state(src, t, split_rows):
-        if not split_rows:
-            moves.append(
-                remote(src, state.at[t], st_send.at[t, 0], st_recv.at[t, 0], prev, me)
+    def eight(c):
+        return pl.ds(pl.multiple_of(c * 8, 8), 8)
+
+    def state_moves(t):
+        if t == 0:
+            to = mx * Z + 1 + mz // 2
+            return [
+                remote(
+                    own.at[:, :, pl.ds(c * HALF, HALF)],
+                    state.at[0, mz % 2, :, eight(core), :],
+                    st_send.at[0, c],
+                    st_recv.at[0, (mz % 2) * 2 + core],
+                    prev,
+                    dev(to, c),
+                )
+                for c in range(2)
+            ]
+        if t < STEPS - 1:
+            return [
+                remote(fresh.at[t - 1], state.at[t], st_send.at[t, 0], st_recv.at[t, 0], prev, me)
+            ]
+        return [
+            remote(
+                fresh.at[t - 1, q, :, pl.ds(c * 8, 8), :],
+                state.at[t, 0, :, eight(core), :],
+                st_send.at[t, q * 2 + c],
+                st_recv.at[t, core],
+                prev,
+                dev(mx * Z + 2 * (mz - 1) + q, c),
             )
-            moves[-1].start()
-            return
-        for c in range(2):
-            moves.append(
+            for q in range(2)
+            for c in range(2)
+        ]
+
+    def state_arrived(t):
+        if t == 0:
+            for q in range(2):
+                for c in range(2):
+                    remote(
+                        own.at[:, :, pl.ds(0, HALF)],
+                        state.at[0, q, :, pl.ds(c * 8, 8), :],
+                        st_send.at[0, 0],
+                        st_recv.at[0, q * 2 + c],
+                        s,
+                        me,
+                    ).wait_recv()
+        elif t < STEPS - 1:
+            remote(
+                fresh.at[t - 1], state.at[t], st_send.at[t, 0], st_recv.at[t, 0], s, me
+            ).wait_recv()
+        else:
+            for c in range(2):
                 remote(
-                    src.at[:, :, pl.ds(c * HALF, HALF)] if t == 0 else src.at[:, pl.ds(c * 8, 8), :],
-                    state.at[t, :, pl.ds(pl.multiple_of(core * 8, 8), 8), :],
-                    st_send.at[t, c],
-                    st_recv.at[t, core],
-                    prev,
-                    dev(chip, c),
-                )
-            )
-            moves[-1].start()
+                    fresh.at[t - 1, 0, :, pl.ds(c * 8, 8), :],
+                    state.at[t, 0, :, pl.ds(c * 8, 8), :],
+                    st_send.at[t, 0],
+                    st_recv.at[t, c],
+                    s,
+                    me,
+                ).wait_recv()
+
+    def updated(t, q):
+        for z_of in range(Z):
+            remote(
+                line.at[t, rows_of(0), :],
+                parts.at[t, q, z_of],
+                rs_send.at[t, 0],
+                rs_recv.at[t, q, z_of],
+                s,
+                me,
+            ).wait_recv()
+        grads = jnp.sum(parts[t, q].astype(jnp.float32), axis=0)
+        momentum = inertia * state[t, q, 1] + FACTOR * grads
+        return state[t, q, 0] - item_rate * momentum, momentum
 
     for t in range(STEPS):
         last = t == STEPS - 1
@@ -234,15 +290,19 @@
 
         tiles = [pl.ds(i * TILE, TILE) for i in range(USERS // TILE)]
         if t == 0:
-            pass_state(own, 0, True)
+            for copy in state_moves(0):
+                copy.start()
             for r in tiles:
                 score[r, :] = dot(u[core, r, :], w[t, core], NT)
         else:
             for r in tiles:
                 score[r, :] = dot(u[core, r, :], w[t, core], NT)
             collect_passed(t, place)
-            pass_state(fresh.at[t - 1], t, last)
-            finish(sends + passed)
+
+            @pl.when(middle)
+            def _(t=t):
+                for copy in state_moves(t):
+                    copy.start()
         for r in tiles:
             total = score[r, :] + dot(u[other, r, :], w[t, other], NT)
             tile = x[t, r, :].astype(jnp.float32)
@@ -316,61 +376,75 @@
             gives[(2, 1, 3).index(i + 1)].wait_recv()
             total += along_x[t, i].astype(jnp.float32)
         line[t] = total.astype(jnp.bfloat16)
-        for dz in (0, 1, 3, 2):
-            z_of = (mz + dz) % Z
+        if last:
+            to_owners = [(z_of, 0, z_of) for z_of in range(Z)]
+        else:
+            to_owners = [(2 * (m - 1) + q, q, m) for q in range(2) for m in (1, 2)]
+        for i, (z_of, q, owner) in enumerate(to_owners):
             gives.append(
                 remote(
-                    line.at[t, rows_of(z_of), :],
-                    parts.at[t, mz],
-                    rs_send.at[t, dz],
-                    rs_recv.at[t, mz],
+                    line.at[t, pl.ds(z_of * ROWS, ROWS), :],
+                    parts.at[t, q, mz],
+                    rs_send.at[t, i],
+                    rs_recv.at[t, q, mz],
                     prev,
-                    dev(mx * Z + z_of, core),
+                    dev(mx * Z + owner, core),
                 )
             )
             gives[-1].start()
-        if t == 0 or last:
-            for c in range(2):
-                remote(
-                    own.at[:, :, pl.ds(c * HALF, HALF)],
-                    state.at[t, :, pl.ds(c * 8, 8), :],
-                    st_send.at[t, c],
-                    st_recv.at[t, c],
-                    s,
-                    me,
-                ).wait_recv()
-        else:
-            remote(
-                fresh.at[t], state.at[t], st_send.at[t, 0], st_recv.at[t, 0], s, me
-            ).wait_recv()
-        for z_of in range(Z):
-            remote(
-                line.at[t, rows_of(0), :],
-                parts.at[t, z_of],
-                rs_send.at[t, 0],
-                rs_recv.at[t, z_of],
-                s,
-                me,
-            ).wait_recv()
-        grads = jnp.sum(parts[t].astype(jnp.float32), axis=0)
-        momentum = inertia * state[t, 1] + FACTOR * grads
-        items = state[t, 0] - item_rate * momentum
+        groups = [(dx, m, q) for q in range(2) for dx in (2, 1, 3, 0) for m in (1, 2)]
         if last:
+            state_arrived(t)
+            items, momentum = updated(t, 0)
             for h in range(2):
                 items_out[:, h * HALF : h * HALF + HALF] = items[h * 8 : h * 8 + 8]
                 momentum_out[:, h * HALF : h * HALF + HALF] = momentum[h * 8 : h * 8 + 8]
         else:
-            w[t + 1, core, rows_of(chip), :] = items.astype(jnp.bfloat16)
 
             def place(c, k, t=t + 1):
                 return w.at[t, c, rows_of(k), :]
 
-            sends, passed, pass_on = spread(t + 1, place)
-            fresh[t, 0] = items
-            fresh[t, 1] = momentum
-            collect(t + 1, place, pass_on)
-        moves += [*gives, *swaps.values()]
-    finish(moves)
+            @pl.when(middle)
+            def _(t=t, place=place):
+                state_arrived(t)
+                for q in range(2):
+                    items, momentum = updated(t, q)
+                    k = mx * Z + 2 * (mz - 1) + q
+                    w[t + 1, core, rows_of(k), :] = items.astype(jnp.bfloat16)
+                    spread(t + 1, q, place, k)
+                    pass_on(t + 1, place, k)
+                    fresh[t, q, 0] = items
+                    fresh[t, q, 1] = momentum
+
+            for dx, m, q in groups[::-1][8:] + groups[::-1][:8]:
+                x_of = (mx + dx) % X
+                k = x_of * Z + 2 * (m - 1) + q
+
+                def take_in(k=k, t=t, place=place):
+                    arrived(t + 1, place, k)
+                    pass_on(t + 1, place, k)
+
+                if dx == 0:
+                    pl.when(mz != m)(take_in)
+                else:
+                    take_in()
+        finish([*gives, *swaps.values()])
+
+    finish(state_moves(0))
+
+    @pl.when(middle)
+    def _():
+        for t in range(1, STEPS):
+            finish(state_moves(t))
+            for q in range(2):
+                for dx, dz in far[:-1]:
+                    mine = w.at[t, core, rows_of(0), :]
+                    remote(
+                        mine, mine, ag_send.at[t, q, dx * Z + dz], ag_recv.at[t, 0], s, me
+                    ).wait_send()
+
+    for t in range(1, STEPS):
+        finish_passed(t, lambda c, k, t=t: w.at[t, c, rows_of(k), :])
 
 
 def write_out(users, items, momentum, users_out, items_out, momentum_out, sem):
@@ -420,11 +494,11 @@
             pltpu.VMEM((STEPS, BLOCK, HALF), bf16),
             pltpu.VMEM((STEPS, X - 1, Z * ROWS, HALF), bf16),
             pltpu.VMEM((STEPS, Z * ROWS, HALF), bf16),
-            pltpu.VMEM((STEPS, Z, ROWS, HALF), bf16),
-            pltpu.VMEM((STEPS, 2, ROWS, HALF), f32),
-            pltpu.VMEM((STEPS, 2, ROWS, HALF), f32),
+            pltpu.VMEM((STEPS, 2, Z, ROWS, HALF), bf16),
+            pltpu.VMEM((STEPS, 2, 2, ROWS, HALF), f32),
+            pltpu.VMEM((STEPS, 2, 2, ROWS, HALF), f32),
             dma((5,)),
-            dma((STEPS, CHIPS)),
+            dma((STEPS, 2, CHIPS)),
             dma((STEPS, CHIPS)),
             dma((STEPS, CHIPS)),
             dma((STEPS, CHIPS)),
@@ -433,9 +507,9 @@
             dma((STEPS, X - 1)),
             dma((STEPS, X - 1)),
             dma((STEPS, Z)),
-            dma((STEPS, Z)),
-            dma((STEPS, 2)),
-            dma((STEPS, 2)),
+            dma((STEPS, 2, Z)),
+            dma((STEPS, 4)),
+            dma((STEPS, 4)),
         ],
         compiler_params=pltpu.CompilerParams(
             collective_id=0, has_side_effects=True, vmem_limit_bytes=48 * 1024 * 1024

time: 85.7 us -> 85.7 us (level)
  the two profiles are of different devices: /device:TPU:1 before, /device:TPU:24 now
where the time goes in v5:
time: 85.7 us; the launch traced here: 85.6 us
  Pallas kernels  84.9 us (99%)
    pallas_call x1, Pallas kernels, local(): pl.pallas_call(kernel, out_shape=(pltpu.VMEM(users.shape, bf16), pltpu.VM...  83.9 us

profile of v5, /device:TPU:24, one launch (start us, length us, event | category | flops | bytes accessed | tf_op | source)
XLA Modules:
  0.0 85.6 jit_solution(6495092453885939496)
XLA Ops:
  0.6 83.9 %shard_map.67 = (bf16[1024,512]{1,0:T(8,128)(2,1)S(1)}, f32[8,512]{1,0:T(8,128)S(1)}, f32[8,512]{1,0:T(8,128)S(1)}) custom-call(bf16[1024,512]{1,0:T(8,128)(2,1)} %users_in.1, f32[8,512]{1,0:T(8,128)} %items_in.1, f32[8,512]{1,0:T(8,128)} %momentum_in.1, bf16[1024,4,256]{2,1,0:T(4,128)(2,1)} %ratings_in.1), custom_call_target="tpu_custom_call" | custom-call | flops 3221225472 | bytes 4194304 | tf_op jit(solution)/shard_map/pallas_call | solution.py:470
  84.6 1.0 %shard_map.68 = (bf16[1024,512]{1,0:T(8,128)(2,1)}, f32[8,512]{1,0:T(8,128)}, f32[8,512]{1,0:T(8,128)}) custom-call(bf16[1024,512]{1,0:T(8,128)(2,1)S(1)} %get-tuple-element.6.users, f32[8,512]{1,0:T(8,128)S(1)} %get-tuple-element.7.items, f32[8,512]{1,0:T(8,128)S(1)} %get-tuple-element.8.momentum), custom_call_target="tpu_custom_call" | custom-call | tf_op jit(solution)/shard_map/pallas_call | solution.py:524
